TPU v7x, 256 devices: a whole 4x4x8 slice. The times are simulated.
256 devices in a mesh: rows: 8 (over x, core), cols: 32 (over y, z).
Axes of the slice: x: 4, y: 4, z: 8, core: 2. Of those that a mesh axis runs over, the one named last changes fastest.
Arguments:
- blocks: bfloat16 [12288, 256, 256], P(('rows', 'cols')), may hold values from 0 to 0.0012969971
- block_row: int32 [12288], P(('rows', 'cols')), may hold values from 0 to 31
- block_col: int32 [12288], P(('rows', 'cols')), may hold values from 0 to 127
- block_count: int32 [256], P(('rows', 'cols')), may hold values from 12 to 48, as said below
- primal: float32 [1048576], P('cols'), may hold values from 0 to 1
- dual: float32 [65536], P('rows'), may hold values from 0 to 2
- cost: float32 [1048576], P('cols'), may hold values from 0.5 to 5
- demand: float32 [65536], P('rows'), may hold values from 0.05 to 5
- step: float32 [1], replicated, may hold values from 0.3 to 0.6
- fresh_pattern_blocks: bfloat16 [8192, 256, 256], P(('rows', 'cols')), may hold values from 0 to 0.0078125
- fresh_block_row: int32 [8192], P(('rows', 'cols')), may hold values from 0 to 255
- fresh_block_column: int32 [8192], P(('rows', 'cols')), may hold values from 0 to 31
- fresh_pattern_cost: float32 [2097152], P(('rows', 'cols')), may hold values from 0.5 to 5
Outputs:
- primal_out: float32 [1048576], P('cols')
- dual_out: float32 [65536], P('rows')
- reduced: float32 [2097152], P(('rows', 'cols'))
Inputs may be any that keep to these rules, and one draw needn't show every extreme that they name: `block_count`: at least a quarter of the slots are live on every device, and some device has all 48 live.
All inputs are finite; a program needn't handle non-finite values.
Results may differ from a plain program's by a relative error of at most 0.0003.
Values sent between devices are 32-bit elements; how exact they have to be, the bound alone decides.
A program may use at most 64 MiB of HBM per device.

v0:
```python
import jax
import jax.numpy as jnp
from jax import lax
from jax.sharding import PartitionSpec as P

ITERS = 2


def block_contribution(blk, row_hot, col_hot, alive, vec, forward):
    HI = lax.Precision.HIGHEST
    size = blk.shape[1]
    if forward:
        pieces = jnp.dot(col_hot, vec.reshape(col_hot.shape[1], size), precision=HI)
        prod = jnp.einsum(
            "sij,sj->si", blk, pieces, precision=HI, preferred_element_type=jnp.float32
        )
        prod = prod * alive[:, None]
        return jnp.dot(row_hot.T, prod, precision=HI).reshape(-1)
    pieces = jnp.dot(row_hot, vec.reshape(row_hot.shape[1], size), precision=HI)
    prod = jnp.einsum("sij,si->sj", blk, pieces, precision=HI, preferred_element_type=jnp.float32)
    prod = prod * alive[:, None]
    return jnp.dot(col_hot.T, prod, precision=HI).reshape(-1)


def local(
    blocks,
    block_row,
    block_col,
    block_count,
    primal,
    dual,
    cost,
    demand,
    step,
    fresh_pattern_blocks,
    fresh_block_row,
    fresh_block_column,
    fresh_pattern_cost,
):
    size = blocks.shape[1]
    slots = blocks.shape[0]
    row_count = dual.shape[0] // size
    col_count = primal.shape[0] // size
    alive = (jnp.arange(slots) < block_count[0]).astype(jnp.float32)
    row_hot = (block_row[:, None] == jnp.arange(row_count)[None, :]).astype(jnp.float32)
    col_hot = (block_col[:, None] == jnp.arange(col_count)[None, :]).astype(jnp.float32)

    def apply_local(vec, forward):
        return block_contribution(blocks, row_hot, col_hot, alive, vec, forward)

    cost_sq = jnp.sum(cost * cost)
    demand_sq = jnp.sum(demand * demand)
    cost_total = lax.psum(cost_sq, "cols")
    demand_total = lax.psum(demand_sq, "rows")
    omega = jnp.sqrt(cost_total) / jnp.sqrt(demand_total)
    tau = step[0] / omega
    sigma = step[0] * omega
    current_primal, current_dual = (primal, dual)
    for turn in range(ITERS):
        partial_cols = apply_local(current_dual, False)
        back = lax.psum(partial_cols, "rows")
        primal_next = jnp.maximum(0.0, current_primal - tau * (cost - back))
        fore = lax.psum(apply_local(2.0 * primal_next - current_primal, True), "cols")
        current_dual = jnp.maximum(0.0, current_dual + sigma * (demand - fore))
        current_primal = primal_next
    gathered_duals = lax.all_gather(current_dual, "rows", axis=0, tiled=True)
    total_rows = gathered_duals.shape[0] // size
    new_count = fresh_pattern_cost.shape[0] // size
    fresh_row_onehot = (fresh_block_row[:, None] == jnp.arange(total_rows)[None, :]).astype(
        jnp.float32
    )
    fresh_column_onehot = (fresh_block_column[:, None] == jnp.arange(new_count)[None, :]).astype(
        jnp.float32
    )
    fresh_alive_mask = jnp.ones((fresh_pattern_blocks.shape[0],), jnp.float32)
    reduced_costs = block_contribution(
        fresh_pattern_blocks,
        fresh_row_onehot,
        fresh_column_onehot,
        fresh_alive_mask,
        gathered_duals,
        False,
    )
    return (current_primal, current_dual, fresh_pattern_cost - reduced_costs)


def solution(mesh):
    placed = (
        P(("rows", "cols"), None, None),
        P(("rows", "cols")),
        P(("rows", "cols")),
        P(("rows", "cols")),
        P("cols"),
        P("rows"),
        P("cols"),
        P("rows"),
        P(),
        P(("rows", "cols"), None, None),
        P(("rows", "cols")),
        P(("rows", "cols")),
        P(("rows", "cols")),
    )
    return jax.shard_map(
        local,
        mesh=mesh,
        in_specs=placed,
        out_specs=(P("cols"), P("rows"), P(("rows", "cols"))),
        check_vma=False,
    )
```

profile of v0, /device:TPU:1, one launch (start us, length us, event | category | flops | bytes accessed | tf_op | source)
XLA Modules:
  0.0 500.0 jit_solution(2049090468779974206)
XLA Ops:
  7.2 0.0 all-reduce.3.cloned.1.call-start
  8.0 0.8 reshape.45
  8.8 0.9 convolution_bitcast_fusion.5
  9.7 5.4 %fusion.10 = f32[48,1,256]{2,1,0:T(1,128)S(1)} fusion(bf16[48,256,256]{2,1,0:T(8,128)(2,1)} %param.13, f32[48,256,1]{1,0,2:T(8,128)S(1)} %convolution_bitcast_fusion.5), kind=kOutput, calls=%fused_computation.29 | convolution fusion | flops 37748736 | bytes 6389760 | tf_op jit(solution)/shard_map/sij,si->sj/dot_general | solution.py:20
  15.0 0.3 convolution_bitcast_fusion.1
  15.4 0.7 copy.26
  16.1 0.0 all-reduce.5.cloned.1.call-start
  16.2 0.6 multiply_reduce_fusion
  16.8 0.6 multiply_reduce_fusion.1
  17.4 65.2 %psum.42 = f32[]{:T(128)} all-reduce(f32[]{:T(128)} %multiply_reduce_fusion), channel_id=1, replica_groups=mesh['rows'=8,'cols'=32] {'cols'}, use_global_device_ids=true, to_apply=%region_1.0 | all-reduce | flops 1 | bytes 8 | tf_op jit(solution)/shard_map/psum | solution.py:53
  82.6 27.2 %psum.43 = f32[]{:T(128)} all-reduce(f32[]{:T(128)} %multiply_reduce_fusion.1), channel_id=1, replica_groups=mesh['rows'=8,'cols'=32] {'rows'}, use_global_device_ids=true, to_apply=%region_3.0 | all-reduce | flops 1 | bytes 8 | tf_op jit(solution)/shard_map/psum | solution.py:54
  111.9 0.9 multiply_subtract_fusion.1
  112.9 0.2 convolution_bitcast_fusion.4
  113.1 7.7 %fusion.7 = f32[48,1,256]{2,1,0:T(1,128)S(1)} fusion(bf16[48,256,256]{2,1,0:T(8,128)(2,1)} %param.13, f32[48,256,1]{1,0,2:T(8,128)S(1)} %convolution_bitcast_fusion.4), kind=kOutput, calls=%fused_computation.26 | convolution fusion | flops 37748736 | bytes 6389760 | tf_op jit(solution)/shard_map/sij,sj->si/dot_general | solution.py:14
  120.8 0.3 convolution_bitcast_fusion.9
  121.2 109.9 %psum.45 = f32[8192]{0:T(1024)S(1)} all-reduce(f32[8192]{0:T(1024)S(1)} %bitcast.58), channel_id=1, replica_groups=mesh['rows'=8,'cols'=32] {'cols'}, use_global_device_ids=true, to_apply=%region_5.0 | all-reduce | flops 8192 | bytes 65536 | tf_op jit(solution)/shard_map/psum | solution.py:63
  231.1 0.2 convolution_bitcast_fusion.3
  231.3 5.4 %fusion.4 = f32[48,1,256]{2,1,0:T(1,128)S(1)} fusion(bf16[48,256,256]{2,1,0:T(8,128)(2,1)} %param.13, f32[48,256,1]{1,0,2:T(8,128)S(1)} %convolution_bitcast_fusion.3), kind=kOutput, calls=%fused_computation.23 | convolution fusion | flops 37748736 | bytes 6389760 | tf_op jit(solution)/shard_map/sij,si->sj/dot_general | solution.py:20
  236.7 0.3 convolution_bitcast_fusion
  237.0 0.7 copy.28
  237.8 81.7 %all-reduce.5.cloned.1.call-done = f32[32768]{0:T(1024)} async-done(((f32[32768]{0:T(1024)}), f32[32768]{0:T(1024)}) %all-reduce.5.cloned.1.call-update) | async-done | bytes 131088 | tf_op jit(solution)/shard_map/psum | solution.py:61
  319.4 1.6 multiply_subtract_fusion
  321.1 0.2 convolution_bitcast_fusion.2
  321.3 7.7 %fusion.1 = f32[48,1,256]{2,1,0:T(1,128)S(1)} fusion(bf16[48,256,256]{2,1,0:T(8,128)(2,1)} %param.13, f32[48,256,1]{1,0,2:T(8,128)S(1)} %convolution_bitcast_fusion.2), kind=kOutput, calls=%fused_computation.20 | convolution fusion | flops 37748736 | bytes 6389760 | tf_op jit(solution)/shard_map/sij,sj->si/dot_general | solution.py:14
  329.1 0.3 convolution_bitcast_fusion.8
  329.4 115.6 %psum.47 = f32[8192]{0:T(1024)S(1)} all-reduce(f32[8192]{0:T(1024)S(1)} %bitcast.59), channel_id=1, replica_groups=mesh['rows'=8,'cols'=32] {'cols'}, use_global_device_ids=true, to_apply=%region_7.0 | all-reduce | flops 8192 | bytes 65536 | tf_op jit(solution)/shard_map/psum | solution.py:63
  445.0 42.9 %all_gather.3 = f32[65536]{0:T(1024)S(1)} all-gather(f32[8192]{0:T(1024)S(1)} %add_maximum_fusion), channel_id=1, replica_groups=mesh['rows'=8,'cols'=32] {'rows'}, dimensions={0}, use_global_device_ids=true | all-gather | bytes 294912 | tf_op jit(solution)/shard_map/all_gather | solution.py:66
  488.0 0.1 reshape.53
  488.1 0.2 convolution_bitcast_fusion.7
  488.3 3.9 fusion.14
  492.3 0.3 convolution_bitcast_fusion.6
  492.6 0.6 sub.35
  (32 shorter events, 0.3 us)
Async XLA Ops:
  7.2 7.9 %copy-start.6 = (s32[48]{0:T(128)S(1)}, s32[48]{0:T(128)}, u32[]{:S(2)}) copy-start(s32[48]{0:T(128)} %param.15) | copy-start | bytes 580
  7.2 9.0 %copy-start = (f32[32768]{0:T(1024)S(1)}, f32[32768]{0:T(1024)}, u32[]{:S(2)}) copy-start(f32[32768]{0:T(1024)} %param.19) | copy-start | bytes 393220
  7.2 9.6 %copy-start.1 = (f32[8192]{0:T(1024)S(1)}, f32[8192]{0:T(1024)}, u32[]{:S(2)}) copy-start(f32[8192]{0:T(1024)} %param.20) | copy-start | bytes 98308
  7.2 104.7 %copy-start.4 = (f32[32768]{0:T(1024)S(1)}, f32[32768]{0:T(1024)}, u32[]{:S(2)}) copy-start(f32[32768]{0:T(1024)} %param.17) | copy-start | bytes 393220
  7.2 104.6 %all-reduce.3.cloned.1.call-start = ((), (), s32[]{:S(2)}) async-start(), calls=%async_computation | async-start | bytes 262144 | tf_op jit(solution)/shard_map/psum | solution.py:61
  9.6 111.2 %copy-start.7 = (s32[48]{0:T(128)S(1)}, s32[48]{0:T(128)}, u32[]{:S(2)}) copy-start(s32[48]{0:T(128)} %param.14) | copy-start | bytes 580
  9.6 221.4 %copy-start.3 = (f32[8192]{0:T(1024)S(1)}, f32[8192]{0:T(1024)}, u32[]{:S(2)}) copy-start(f32[8192]{0:T(1024)} %param.18) | copy-start | bytes 98308
  16.1 303.3 %all-reduce.5.cloned.1.call-start = ((), (), s32[]{:S(2)}) async-start(), calls=%async_computation.1 | async-start | bytes 262144 | tf_op jit(solution)/shard_map/psum | solution.py:61
  231.3 256.8 %copy-start.8 = (s32[32]{0:T(128)S(1)}, s32[32]{0:T(128)}, u32[]{:S(2)}) copy-start(s32[32]{0:T(128)} %param.23) | copy-start | bytes 388
  321.0 171.2 %copy-start.9 = (s32[32]{0:T(128)S(1)}, s32[32]{0:T(128)}, u32[]{:S(2)}) copy-start(s32[32]{0:T(128)} %param.24) | copy-start | bytes 388
  321.1 171.5 %copy-start.5 = (f32[8192]{0:T(1024)S(1)}, f32[8192]{0:T(1024)}, u32[]{:S(2)}) copy-start(f32[8192]{0:T(1024)} %param.25) | copy-start | bytes 98308
  445.0 48.2 %copy-start.2 = (f32[8192]{0:T(1024)}, f32[8192]{0:T(1024)S(1)}, u32[]{:S(2)}) copy-start(f32[8192]{0:T(1024)S(1)} %add_maximum_fusion) | copy-start | bytes 98308
Sparse Core Ops, SparseCore 0:
  16.2 66.3 all-reduce.2
  237.9 81.5 all-reduce.4
where the time goes:
time: 500 us
  blocking collectives  361 us (72%)
  waiting for transfers between devices  81.7 us (16%)
  matrix products  33.5 us (7%)
  between operations  17 us (3%)
    psum x2, blocking collectives, local(): lax.psum(apply_local(2.0 * primal_next - current_primal, True), 'cols')  226 us
    psum x2, waiting for transfers between devices, local(): back = lax.psum(partial_cols, 'rows')  81.7 us
    psum x1, blocking collectives, local(): cost_total = lax.psum(cost_sq, 'cols')  65.2 us
    all_gather x1, blocking collectives, local(): gathered_duals = lax.all_gather(current_dual, 'rows', axis=0, tiled=True)  42.9 us
    psum x1, blocking collectives, local(): demand_total = lax.psum(demand_sq, 'rows')  27.2 us
    dot_general x2, matrix products, block_contribution(): jnp.einsum('sij,sj->si', blk, pieces, precision=HI, preferred_element_typ...  15.5 us
    dot_general x3, matrix products, block_contribution(): jnp.einsum('sij,si->sj', blk, pieces, precision=HI, preferred_element_typ...  14.7 us
  transfers between devices with their start and end apart: 2, of which 1 were waited for; matrix products, arithmetic and copies ran while one was open for 0% of the time, Pallas kernels for 0%

commit v1 on v0

v1 whole, which is shorter than its diff:
```python
import jax
import jax.numpy as jnp
from jax import lax
from jax.sharding import PartitionSpec as P
from jax.experimental import pallas as pl
from jax.experimental.pallas import tpu as pltpu

MESH = pl.DeviceIdType.MESH
ITERS = 2
EDGE = 256
LANES = 128
SLOTS = 48
NEW = 32
XN, YN, ZN = 4, 4, 8
PLANE = YN * ZN
COLB = 128
ROWB = 32
CHUNK = 8
BF = jnp.bfloat16
F32 = jnp.float32
LOADS = 4


def split3(v):
    hi = v.astype(BF).astype(F32)
    rest = v - hi
    mid = rest.astype(BF).astype(F32)
    return hi, mid, rest - mid


def piece_tile(ref, at, lane_row):
    v = jnp.concatenate([ref[pl.ds(at, 1), :], ref[pl.ds(at + 1, 1), :]], axis=1)
    v = jnp.broadcast_to(v, (8, EDGE))
    hi, mid, lo = split3(v)
    tile = jnp.where(lane_row == 0, hi, jnp.where(lane_row == 1, mid, lo))
    return jnp.where(lane_row < 3, tile, 0.0).astype(BF)


def products(count, unroll, vec_ref, start_of, blk_ref, out_ref, transposed):
    lane_row = lax.broadcasted_iota(jnp.int32, (8, EDGE), 0)
    dims = (((1,), (1,)), ((), ())) if transposed else (((1,), (0,)), ((), ()))

    def step(i, _):
        for u in range(unroll):
            s = i * unroll + u
            tile = piece_tile(vec_ref, start_of(s), lane_row)
            res = lax.dot_general(tile, blk_ref[s], dims, preferred_element_type=F32)
            out_ref[pl.ds(s, 1), :] = jnp.sum(res, axis=0, keepdims=True)
        return 0

    lax.fori_loop(0, count // unroll, step, 0)


def scatter(hot, prod):
    out = None
    for part in split3(prod):
        term = jnp.dot(hot, part.astype(BF), preferred_element_type=F32)
        out = term if out is None else out + term
    return out


def put_pairs(ref, val, at=0):
    n = val.shape[0]
    ref[pl.ds(at, n, stride=2), :] = val[:, :LANES]
    ref[pl.ds(at + 1, n, stride=2), :] = val[:, LANES:]


def kernel(
    brow_s, bcol_s, cnt_s, frow_s, step_s,
    bcol_v, brow_v, fcol_v,
    primal, dual, cost, demand, fcost,
    blocks, fresh,
    primal_o, dual_o, reduced_o,
    blk, frs, prod, pbuf, meta, metabuf, dense, sib, costrow, costbuf,
    xbar, xcur, prodf, part, rsbuf, ybuf, yall, prodn, priced,
    load_sem, fresh_sem, px_send, px_recv, meta_send, meta_recv, cost_send, cost_recv,
    sib_send, sib_recv, rs_send, rs_recv, ag_send, ag_recv, fx_send, fx_recv, fs_send, fs_recv,
):
    r = lax.axis_index("rows")
    c = lax.axis_index("cols")
    x, core = r // 2, lax.rem(r, 2)
    y, z = c // ZN, lax.rem(c, ZN)
    per = SLOTS // LOADS

    def load(i):
        return pltpu.make_async_copy(
            blocks.at[pl.ds(i * per, per)], blk.at[pl.ds(i * per, per)], load_sem.at[i]
        )

    fresh_copy = pltpu.make_async_copy(fresh, frs, fresh_sem)
    for i in range(LOADS):
        load(i).start()

    def plane_peer(k):
        return lax.rem(y + k // ZN, YN), lax.rem(z + lax.rem(k, ZN), ZN)

    def x_peer(d):
        return (lax.rem(x + d, XN) * 2 + core, c)

    sibling = (x * 2 + 1 - core, c)

    barrier = pltpu.get_barrier_semaphore()

    def greet(k, _):
        ty, tz = plane_peer(k)
        pl.semaphore_signal(barrier, inc=1, device_id=(r, ty * ZN + tz), device_id_type=MESH)
        return 0

    def greet_x(d, _):
        pl.semaphore_signal(barrier, inc=1, device_id=x_peer(d), device_id_type=MESH)
        return 0

    lax.fori_loop(1, PLANE, greet, 0)
    lax.fori_loop(1, XN, greet_x, 0)
    pl.semaphore_signal(barrier, inc=1, device_id=sibling, device_id_type=MESH)

    lanes = lax.broadcasted_iota(jnp.int32, (1, SLOTS), 1)
    alive = lanes < cnt_s[0]
    my_cols = jnp.where(alive, bcol_v[...], -1)
    my_rows = jnp.where(alive, brow_v[...], -1)
    row_hot = (lax.broadcasted_iota(jnp.int32, (ROWB, SLOTS), 0) == my_rows).astype(F32).astype(BF)
    col_ids = lax.broadcasted_iota(jnp.int32, (COLB, SLOTS), 0).astype(F32)

    def col_hot(cols):
        return (col_ids == cols).astype(F32).astype(BF)

    dem_sq = jnp.sum(demand[...] * demand[...], axis=0, keepdims=True)
    meta[...] = jnp.zeros_like(meta)
    meta[0:1, 0:SLOTS] = my_cols.astype(F32)
    meta[1:2, :] = dem_sq
    costrow[...] = jnp.sum(cost[...] * cost[...], axis=0, keepdims=True)

    def back_products(vec_ref, out_ref):
        products(SLOTS, 12, vec_ref, lambda s: 2 * brow_s[s], blk, out_ref, False)

    for i in range(LOADS):
        load(i).wait()
    fresh_copy.start()

    back_products(dual, prod.at[0])
    pl.semaphore_wait(barrier, PLANE - 1 + XN - 1 + 1)

    my_chunk = lax.rem(y, 2) * 4 + lax.rem(z, 4)
    my_at = pl.multiple_of(my_chunk * CHUNK, CHUNK)
    tau = sigma = None
    for it in range(ITERS):
        def send_products(d, _, it=it):
            pltpu.make_async_remote_copy(
                src_ref=prod.at[it], dst_ref=pbuf.at[it, d - 1],
                send_sem=px_send.at[it], recv_sem=px_recv.at[it, d - 1],
                device_id=x_peer(d), device_id_type=MESH,
            ).start()
            return 0

        if it == 0:
            def send_meta(d, _):
                pltpu.make_async_remote_copy(
                    src_ref=meta, dst_ref=metabuf.at[d - 1],
                    send_sem=meta_send, recv_sem=meta_recv,
                    device_id=x_peer(d), device_id_type=MESH,
                ).start()
                return 0

            lax.fori_loop(1, XN, send_meta, 0)
        lax.fori_loop(1, XN, send_products, 0)
        if it == 0:
            def send_cost(k, _):
                ty, tz = plane_peer(k)
                pltpu.make_async_remote_copy(
                    src_ref=costrow, dst_ref=costbuf.at[k],
                    send_sem=cost_send, recv_sem=cost_recv,
                    device_id=(r, ty * ZN + tz), device_id_type=MESH,
                ).start()
                return 0

            lax.fori_loop(1, PLANE, send_cost, 0)
        total = scatter(col_hot(my_cols.astype(F32)), prod[it])
        if it == 0:
            pltpu.make_async_copy(metabuf, metabuf, meta_recv).wait()
        for d in range(XN - 1):
            pltpu.make_async_copy(pbuf.at[it, d], pbuf.at[it, d], px_recv.at[it, d]).wait()
            total = total + scatter(col_hot(metabuf[d, 0:1, 0:SLOTS]), pbuf[it, d])
        put_pairs(dense.at[it], total)
        if it == 0:
            dem4 = dem_sq + metabuf[0, 1:2, :] + metabuf[1, 1:2, :] + metabuf[2, 1:2, :]
            dense[it, 2 * COLB:, :] = jnp.broadcast_to(dem4, (8, LANES))
        to_sibling = pltpu.make_async_remote_copy(
            src_ref=dense.at[it], dst_ref=sib.at[it],
            send_sem=sib_send.at[it], recv_sem=sib_recv.at[it],
            device_id=sibling, device_id_type=MESH,
        )
        to_sibling.start()
        if it == 0:
            pltpu.make_async_copy(costbuf.at[pl.ds(1, PLANE - 1)], costbuf.at[pl.ds(1, PLANE - 1)], cost_recv).wait()
            costbuf[0] = costrow[...]
            cost_total = jnp.sum(jnp.sum(costbuf[...], axis=0), axis=1, keepdims=True)
        to_sibling.wait_recv()
        if it == 0:
            dem_total = jnp.sum(dem4 + sib[it, 2 * COLB:2 * COLB + 1, :], axis=1, keepdims=True)
            omega = jnp.sqrt(cost_total) / jnp.sqrt(dem_total)
            tau = step_s[0] / omega
            sigma = step_s[0] * omega
        was = primal[...] if it == 0 else xcur[...]
        back = dense[it, 0:2 * COLB, :] + sib[it, 0:2 * COLB, :]
        now = jnp.maximum(0.0, was - tau * (cost[...] - back))
        xbar[...] = 2.0 * now - was
        if it == ITERS - 1:
            primal_o[...] = now
        else:
            xcur[...] = now

        products(SLOTS, 12, xbar, lambda s: 2 * bcol_s[s], blk, prodf, True)
        put_pairs(part.at[it], scatter(row_hot, prodf[...]))

        def send_chunk(k, _, it=it):
            ty, tz = plane_peer(k)
            at = pl.multiple_of((lax.rem(ty, 2) * 4 + lax.rem(tz, 4)) * CHUNK, CHUNK)
            pltpu.make_async_remote_copy(
                src_ref=part.at[it, pl.ds(at, CHUNK)], dst_ref=rsbuf.at[it, k],
                send_sem=rs_send.at[it], recv_sem=rs_recv.at[it],
                device_id=(r, ty * ZN + tz), device_id_type=MESH,
            ).start()
            return 0

        lax.fori_loop(1, PLANE, send_chunk, 0)
        mine = part[it, pl.ds(my_at, CHUNK), :]
        rs_all = rsbuf.at[it, pl.ds(1, PLANE - 1)]
        pltpu.make_async_copy(rs_all, rs_all, rs_recv.at[it]).wait()
        fore = mine + jnp.sum(rsbuf[it, 1:PLANE], axis=0)
        y_was = dual[pl.ds(my_at, CHUNK), :] if it == 0 else ybuf[it - 1, pl.ds(my_at, CHUNK), :]
        y_now = jnp.maximum(0.0, y_was + sigma * (demand[pl.ds(my_at, CHUNK), :] - fore))
        held = ybuf.at[it] if it < ITERS - 1 else yall.at[core, x]
        held[pl.ds(my_at, CHUNK), :] = y_now

        def send_dual(k, _, it=it, held=held):
            ty = lax.rem(y + k // 4, YN)
            tz = lax.rem(z + lax.rem(k, 4) + ZN - 1, ZN)
            pltpu.make_async_remote_copy(
                src_ref=held.at[pl.ds(my_at, CHUNK)], dst_ref=held.at[pl.ds(my_at, CHUNK)],
                send_sem=ag_send.at[it], recv_sem=ag_recv.at[it],
                device_id=(r, ty * ZN + tz), device_id_type=MESH,
            ).start()
            return 0

        send_dual(0, 0)
        lax.fori_loop(2, 8, send_dual, 0)
        seven = held.at[pl.ds(0, 7 * CHUNK)]
        pltpu.make_async_copy(seven, seven, ag_recv.at[it]).wait()
        if it < ITERS - 1:
            back_products(ybuf.at[it], prod.at[it + 1])

    own = yall.at[core, x]

    def send_rows(d, _):
        pltpu.make_async_remote_copy(
            src_ref=own, dst_ref=own,
            send_sem=fx_send, recv_sem=fx_recv,
            device_id=x_peer(d), device_id_type=MESH,
        ).start()
        return 0

    lax.fori_loop(1, XN, send_rows, 0)
    dual_o[...] = own[...]
    fresh_copy.wait()
    three = yall.at[core, pl.ds(0, XN - 1)]
    pltpu.make_async_copy(three, three, fx_recv).wait()
    half = pltpu.make_async_remote_copy(
        src_ref=yall.at[core], dst_ref=yall.at[core],
        send_sem=fs_send, recv_sem=fs_recv,
        device_id=sibling, device_id_type=MESH,
    )
    half.start()
    half.wait_recv()

    yflat = yall.reshape(2 * XN * 2 * ROWB, LANES)

    def new_at(s):
        block = frow_s[s]
        rr = block // ROWB
        return lax.rem(rr, 2) * (XN * 2 * ROWB) + (rr // 2) * (2 * ROWB) + lax.rem(block, ROWB) * 2

    products(NEW, 8, yflat, new_at, frs, prodn, False)
    new_hot = (lax.broadcasted_iota(jnp.int32, (NEW, NEW), 0) == fcol_v[...]).astype(F32).astype(BF)
    put_pairs(priced, scatter(new_hot, prodn[...]))
    reduced_o[...] = fcost[...] - priced[...]

    half.wait_send()
    pltpu.make_async_copy(three, three, fx_send).wait()
    meta3 = metabuf
    pltpu.make_async_copy(meta3, meta3, meta_send).wait()
    cost31 = costbuf.at[pl.ds(1, PLANE - 1)]
    pltpu.make_async_copy(cost31, cost31, cost_send).wait()
    for it in range(ITERS):
        pltpu.make_async_copy(pbuf.at[it], pbuf.at[it], px_send.at[it]).wait()
        pltpu.make_async_copy(sib.at[it], sib.at[it], sib_send.at[it]).wait()
        rs_all = rsbuf.at[it, pl.ds(1, PLANE - 1)]
        pltpu.make_async_copy(rs_all, rs_all, rs_send.at[it]).wait()
        seven = ybuf.at[it, pl.ds(0, 7 * CHUNK)]
        pltpu.make_async_copy(seven, seven, ag_send.at[it]).wait()


def local(
    blocks, block_row, block_col, block_count, primal, dual, cost, demand, step,
    fresh_pattern_blocks, fresh_block_row, fresh_block_column, fresh_pattern_cost,
):
    smem = pl.BlockSpec(memory_space=pltpu.SMEM)
    vmem = pl.BlockSpec(memory_space=pltpu.VMEM)
    hbm = pl.BlockSpec(memory_space=pl.ANY)
    dma = pltpu.SemaphoreType.DMA
    rows2 = lambda v: v.reshape(-1, LANES)
    outs = pl.pallas_call(
        kernel,
        out_shape=(
            jax.ShapeDtypeStruct((2 * COLB, LANES), F32),
            jax.ShapeDtypeStruct((2 * ROWB, LANES), F32),
            jax.ShapeDtypeStruct((2 * NEW, LANES), F32),
        ),
        in_specs=[smem] * 5 + [vmem] * 8 + [hbm] * 2,
        out_specs=(vmem, vmem, vmem),
        scratch_shapes=[
            pltpu.VMEM((SLOTS, EDGE, EDGE), BF),
            pltpu.VMEM((NEW, EDGE, EDGE), BF),
            pltpu.VMEM((ITERS, SLOTS, EDGE), F32),
            pltpu.VMEM((ITERS, XN - 1, SLOTS, EDGE), F32),
            pltpu.VMEM((8, LANES), F32),
            pltpu.VMEM((XN - 1, 8, LANES), F32),
            pltpu.VMEM((ITERS, 2 * COLB + 8, LANES), F32),
            pltpu.VMEM((ITERS, 2 * COLB + 8, LANES), F32),
            pltpu.VMEM((1, LANES), F32),
            pltpu.VMEM((PLANE, 1, LANES), F32),
            pltpu.VMEM((2 * COLB, LANES), F32),
            pltpu.VMEM((2 * COLB, LANES), F32),
            pltpu.VMEM((SLOTS, EDGE), F32),
            pltpu.VMEM((ITERS, 2 * ROWB, LANES), F32),
            pltpu.VMEM((ITERS, PLANE, CHUNK, LANES), F32),
            pltpu.VMEM((ITERS, 2 * ROWB, LANES), F32),
            pltpu.VMEM((2, XN, 2 * ROWB, LANES), F32),
            pltpu.VMEM((NEW, EDGE), F32),
            pltpu.VMEM((2 * NEW, LANES), F32),
            dma((LOADS,)), dma,
            dma((ITERS,)), dma((ITERS, XN - 1)), dma, dma, dma, dma,
            dma((ITERS,)), dma((ITERS,)), dma((ITERS,)), dma((ITERS,)),
            dma((ITERS,)), dma((ITERS,)), dma, dma, dma, dma,
        ],
        compiler_params=pltpu.CompilerParams(
            collective_id=0, has_side_effects=True, vmem_limit_bytes=40 * 2**20
        ),
    )(
        block_row, block_col, block_count, fresh_block_row, step,
        block_col.reshape(1, -1), block_row.reshape(1, -1), fresh_block_column.reshape(1, -1),
        rows2(primal), rows2(dual), rows2(cost), rows2(demand), rows2(fresh_pattern_cost),
        blocks, fresh_pattern_blocks,
    )
    return tuple(o.reshape(-1) for o in outs)


def solution(mesh):
    both = ("rows", "cols")
    placed = (
        P(both, None, None), P(both), P(both), P(both),
        P("cols"), P("rows"), P("cols"), P("rows"), P(),
        P(both, None, None), P(both), P(both), P(both),
    )
    return jax.shard_map(
        local, mesh=mesh, in_specs=placed,
        out_specs=(P("cols"), P("rows"), P(both)), check_vma=False,
    )
```

time: 500 us -> 76.9 us (0.15)
  blocking collectives: 361 us -> 0 us
  waiting for transfers between devices: 81.7 us -> 0 us
  Pallas kernels: 0 us -> 60.9 us
  matrix products: 33.5 us -> 0 us
  between operations: 17 us -> 1.95 us
  local copies, waits for them, and re-layouts: 2.48 us -> 13.6 us
    psum x4 -> x0, blocking collectives: 318 us -> none  [the longest x2 226 us: local(): lax.psum(apply_local(2.0 * primal_next - current_primal, True), 'cols')]
    psum x2 -> x0, waiting for transfers between devices: 81.7 us -> none  [local(): back = lax.psum(partial_cols, 'rows')]
    pallas_call x0 -> x1, Pallas kernels: none -> 60.9 us  [local(): pl.pallas_call(kernel, out_shape=(jax.ShapeDtypeStruct((2 * COLB, LANES),...]
    all_gather x1 -> x0, blocking collectives: 42.9 us -> none  [local(): gathered_duals = lax.all_gather(current_dual, 'rows', axis=0, tiled=True)]
    dot_general x15 -> x0, matrix products: 33.5 us -> none  [the longest x2 15.5 us: block_contribution(): jnp.einsum('sij,sj->si', blk, pieces, precision=HI, preferred_element_typ...]
    unnamed x25, local copies, waits for them, and re-layouts: 1.55 us -> 13.6 us
  transfers between devices with their start and end apart: 2 -> 0, of which waited for: 1 -> 0; matrix products, arithmetic and copies ran while one was open for 0% -> 0% of each run, Pallas kernels for 0% -> 0%
where the time goes in v1:
time: 76.9 us; the launch traced here: 76.5 us
  Pallas kernels  60.9 us (79%)
  local copies, waits for them, and re-layouts  13.6 us (18%)
  between operations  1.95 us (3%)
    pallas_call x1, Pallas kernels, local(): pl.pallas_call(kernel, out_shape=(jax.ShapeDtypeStruct((2 * COLB, LANES),...  60.9 us
    unnamed x25, local copies, waits for them, and re-layouts  13.6 us

profile of v1, /device:TPU:1, one launch (start us, length us, event | category | flops | bytes accessed | tf_op | source)
XLA Modules:
  0.0 76.5 jit_solution(2934839616666254105)
XLA Ops:
  1.9 0.0 copy-start
  1.9 2.8 %copy-done = bf16[48,256,256]{2,1,0:T(8,128)(2,1)S(1)} copy-done((bf16[48,256,256]{2,1,0:T(8,128)(2,1)S(1)}, bf16[48,256,256]{2,1,0:T(8,128)(2,1)}, u32[]{:S(2)}) %copy-start) | copy-done | bytes 6291480
  4.7 0.0 copy-start.1
  4.7 2.2 %copy-done.1 = bf16[32,256,256]{2,1,0:T(8,128)(2,1)S(1)} copy-done((bf16[32,256,256]{2,1,0:T(8,128)(2,1)S(1)}, bf16[32,256,256]{2,1,0:T(8,128)(2,1)}, u32[]{:S(2)}) %copy-start.1) | copy-done | bytes 4194328
  6.9 0.0 copy-start.2
  6.9 0.9 %copy-done.2 = f32[32768]{0:T(1024)S(1)} copy-done((f32[32768]{0:T(1024)S(1)}, f32[32768]{0:T(1024)}, u32[]{:S(2)}) %copy-start.2) | copy-done | bytes 131096
  7.8 0.0 copy-start.3
  7.8 0.9 %copy-done.3 = f32[32768]{0:T(1024)S(1)} copy-done((f32[32768]{0:T(1024)S(1)}, f32[32768]{0:T(1024)}, u32[]{:S(2)}) %copy-start.3) | copy-done | bytes 131096
  8.7 0.0 copy-start.4
  8.7 0.8 copy-done.4
  9.5 0.0 copy-start.5
  9.5 0.8 copy-done.5
  10.2 0.0 copy-start.6
  10.2 0.8 copy-done.6
  11.0 0.0 copy-start.7
  11.0 0.7 copy-done.7
  11.6 0.0 copy-start.8
  11.6 0.7 copy-done.8
  12.3 0.0 copy-start.9
  12.3 0.7 copy-done.9
  13.0 0.0 copy-start.10
  13.0 0.7 copy-done.10
  13.6 60.9 %shard_map.148 = (f32[256,128]{1,0:T(8,128)S(1)}, f32[64,128]{1,0:T(8,128)S(1)}, f32[64,128]{1,0:T(8,128)S(1)}) custom-call(s32[48]{0:T(128)S(1)} %copy-done.7, s32[48]{0:T(128)S(1)} %copy-done.8, s32[1]{0:T(128)S(6)} %copy.19.cnt_s, s32[32]{0:T(128)S(1)} %copy-done.9, f32[1]{0:T(128)S(6)} %copy.20.step_s, s32[1,48]{1,0:T(1,128)S(1)} %bitcast.20, ...), custom_call_target="tpu_custom_call" | custom-call | tf_op jit(solution)/shard_map/pallas_call | solution.py:311
  74.6 0.7 copy.21
  75.2 0.6 copy.22
  75.8 0.6 copy.23
Async XLA Ops:
  1.9 2.8 %copy-start = (bf16[48,256,256]{2,1,0:T(8,128)(2,1)S(1)}, bf16[48,256,256]{2,1,0:T(8,128)(2,1)}, u32[]{:S(2)}) copy-start(bf16[48,256,256]{2,1,0:T(8,128)(2,1)} %blocks.1) | copy-start | bytes 18874372
  4.7 2.2 %copy-start.1 = (bf16[32,256,256]{2,1,0:T(8,128)(2,1)S(1)}, bf16[32,256,256]{2,1,0:T(8,128)(2,1)}, u32[]{:S(2)}) copy-start(bf16[32,256,256]{2,1,0:T(8,128)(2,1)} %fresh.1) | copy-start | bytes 12582916
  6.9 0.9 %copy-start.2 = (f32[32768]{0:T(1024)S(1)}, f32[32768]{0:T(1024)}, u32[]{:S(2)}) copy-start(f32[32768]{0:T(1024)} %param.17) | copy-start | bytes 393220
  7.8 0.9 %copy-start.3 = (f32[32768]{0:T(1024)S(1)}, f32[32768]{0:T(1024)}, u32[]{:S(2)}) copy-start(f32[32768]{0:T(1024)} %param.19) | copy-start | bytes 393220
  8.7 0.8 copy-start.4
  9.5 0.8 copy-start.5
  10.2 0.8 copy-start.6
  11.0 0.7 copy-start.7
  11.6 0.7 copy-start.8
  12.3 0.7 copy-start.9
  13.0 0.7 copy-start.10

commit v2 on v1

v2 whole, which is shorter than its diff:
```python
import jax
import jax.numpy as jnp
from jax import lax
from jax.sharding import PartitionSpec as P
from jax.experimental import pallas as pl
from jax.experimental.pallas import tpu as pltpu

MESH = pl.DeviceIdType.MESH
ITERS = 2
EDGE = 256
LANES = 128
SLOTS = 48
NEW = 32
XN, YN, ZN = 4, 4, 8
PLANE = YN * ZN
COLB = 128
ROWB = 32
CHUNK = 8
BF = jnp.bfloat16
F32 = jnp.float32
LOADS = 4
UNROLL = 12
UNROLL_NEW = 8


def split3(v):
    hi = v.astype(BF).astype(F32)
    rest = v - hi
    mid = rest.astype(BF).astype(F32)
    return hi, mid, rest - mid


def piece_tile(ref, at, lane_row):
    v = jnp.concatenate([ref[pl.ds(at, 1), :], ref[pl.ds(at + 1, 1), :]], axis=1)
    v = jnp.broadcast_to(v, (8, EDGE))
    hi, mid, lo = split3(v)
    tile = jnp.where(lane_row == 0, hi, jnp.where(lane_row == 1, mid, lo))
    return jnp.where(lane_row < 3, tile, 0.0).astype(BF)


def products(count, unroll, vec_ref, start_of, blk_ref, out_ref, transposed):
    lane_row = lax.broadcasted_iota(jnp.int32, (8, EDGE), 0)
    dims = (((1,), (1,)), ((), ())) if transposed else (((1,), (0,)), ((), ()))

    def step(i, _):
        for u in range(unroll):
            s = i * unroll + u
            tile = piece_tile(vec_ref, start_of(s), lane_row)
            res = lax.dot_general(tile, blk_ref[s], dims, preferred_element_type=F32)
            out_ref[pl.ds(s, 1), :] = jnp.sum(res, axis=0, keepdims=True)
        return 0

    lax.fori_loop(0, count // unroll, step, 0)


def scatter(hot, prod):
    out = None
    for part in split3(prod):
        term = jnp.dot(hot, part.astype(BF), preferred_element_type=F32)
        out = term if out is None else out + term
    return out


def put_pairs(ref, val, at=0):
    n = val.shape[0]
    ref[pl.ds(at, n, stride=2), :] = val[:, :LANES]
    ref[pl.ds(at + 1, n, stride=2), :] = val[:, LANES:]


def send(src, dst, send_sem, recv_sem, device):
    pltpu.make_async_remote_copy(
        src_ref=src, dst_ref=dst, send_sem=send_sem, recv_sem=recv_sem,
        device_id=device, device_id_type=MESH,
    ).start()


def wait_for(ref, sem):
    pltpu.make_async_copy(ref, ref, sem).wait()


def fetch(src, dst, sem):
    copy = pltpu.make_async_copy(src, dst, sem)
    copy.start()
    return copy


def kernel(
    brow_h, bcol_h, cnt_h, frow_h, step_h, bcolv_h, browv_h, fcolv_h,
    primal_h, dual_h, cost_h, demand_h, fcost_h, blocks, fresh,
    primal_oh, dual_oh, reduced_oh,
    primal_o, dual_o, reduced_o, out_sem,
    brow_s, bcol_s, cnt_s, frow_s, step_s, bcol_v, brow_v, fcol_v,
    primal, dual, cost, demand, fcost,
    blk, frs, prod, pbuf, meta, metabuf, dense, sib, costrow, costbuf,
    xbar, xcur, prodf, part, rsbuf, ybuf, yall, prodn, priced,
    in_sem, load_sem, fresh_sem, px_send, px_recv, meta_send, meta_recv, cost_send, cost_recv,
    sib_send, sib_recv, rs_send, rs_recv, ag_send, ag_recv, fs_send, fs_recv,
):
    r = lax.axis_index("rows")
    c = lax.axis_index("cols")
    x, core = r // 2, lax.rem(r, 2)
    y, z = c // ZN, lax.rem(c, ZN)
    per = SLOTS // LOADS

    first = [
        fetch(src, dst, in_sem.at[i])
        for i, (src, dst) in enumerate([(brow_h, brow_s), (dual_h, dual)])
    ]
    loads = [
        fetch(blocks.at[pl.ds(i * per, per)], blk.at[pl.ds(i * per, per)], load_sem.at[i])
        for i in range(LOADS)
    ]
    pairs = [
        (cnt_h, cnt_s), (bcolv_h, bcol_v), (browv_h, brow_v), (cost_h, cost), (demand_h, demand),
        (step_h, step_s), (bcol_h, bcol_s), (primal_h, primal),
        (frow_h, frow_s), (fcolv_h, fcol_v), (fcost_h, fcost),
    ]
    rest = [fetch(src, dst, in_sem.at[i + 2]) for i, (src, dst) in enumerate(pairs)]

    def plane_peer(j):
        return lax.rem(y + 2 + j // ZN, YN), lax.rem(z + 4 + lax.rem(j, ZN), ZN)

    def x_peer(d):
        return (lax.rem(x + d, XN) * 2 + core, c)

    def each_plane(do):
        lax.fori_loop(0, 20, lambda j, _: (do(j), 0)[1], 0)
        lax.fori_loop(21, PLANE, lambda j, _: (do(j), 0)[1], 0)

    sibling = (x * 2 + 1 - core, c)
    barrier = pltpu.get_barrier_semaphore()

    def greet(device):
        pl.semaphore_signal(barrier, inc=1, device_id=device, device_id_type=MESH)

    def greet_plane(j):
        ty, tz = plane_peer(j)
        greet((r, ty * ZN + tz))

    each_plane(greet_plane)
    lax.fori_loop(1, XN, lambda d, _: (greet(x_peer(d)), 0)[1], 0)
    greet(sibling)

    def back_products(vec_ref, out_ref):
        products(SLOTS, UNROLL, vec_ref, lambda s: 2 * brow_s[s], blk, out_ref, False)

    for copy in first + loads:
        copy.wait()
    fresh_copy = fetch(fresh, frs, fresh_sem)
    back_products(dual, prod.at[0])

    for copy in rest:
        copy.wait()
    lanes = lax.broadcasted_iota(jnp.int32, (1, SLOTS), 1)
    alive = lanes < cnt_s[0]
    my_cols = jnp.where(alive, bcol_v[...], -1)
    my_rows = jnp.where(alive, brow_v[...], -1)
    row_hot = (lax.broadcasted_iota(jnp.int32, (ROWB, SLOTS), 0) == my_rows).astype(F32).astype(BF)
    col_ids = lax.broadcasted_iota(jnp.int32, (COLB, SLOTS), 0).astype(F32)

    def col_hot(cols):
        return (col_ids == cols).astype(F32).astype(BF)

    dem_sq = jnp.sum(demand[...] * demand[...], axis=0, keepdims=True)
    meta[...] = jnp.zeros_like(meta)
    meta[0:1, 0:SLOTS] = my_cols.astype(F32)
    meta[1:2, :] = dem_sq
    costrow[...] = jnp.sum(cost[...] * cost[...], axis=0, keepdims=True)

    pl.semaphore_wait(barrier, PLANE - 1 + XN - 1 + 1)

    my_chunk = lax.rem(y, 2) * 4 + lax.rem(z, 4)
    my_at = pl.multiple_of(my_chunk * CHUNK, CHUNK)
    tau = sigma = None
    for it in range(ITERS):
        def send_products(d, _, it=it):
            if it == 0:
                send(meta, metabuf.at[d - 1], meta_send, meta_recv, x_peer(d))
            send(prod.at[it], pbuf.at[it, d - 1], px_send.at[it], px_recv.at[it, d - 1], x_peer(d))
            return 0

        lax.fori_loop(1, XN, send_products, 0)
        if it == 0:
            def send_cost(j):
                ty, tz = plane_peer(j)
                send(costrow, costbuf.at[j], cost_send, cost_recv, (r, ty * ZN + tz))

            each_plane(send_cost)
        total = scatter(col_hot(my_cols.astype(F32)), prod[it])
        if it == 0:
            wait_for(metabuf, meta_recv)
        for d in (0, 2, 1):
            wait_for(pbuf.at[it, d], px_recv.at[it, d])
            total = total + scatter(col_hot(metabuf[d, 0:1, 0:SLOTS]), pbuf[it, d])
        put_pairs(dense.at[it], total)
        if it == 0:
            dem4 = dem_sq + metabuf[0, 1:2, :] + metabuf[1, 1:2, :] + metabuf[2, 1:2, :]
            dense[it, 2 * COLB:, :] = jnp.broadcast_to(dem4, (8, LANES))
        send(dense.at[it], sib.at[it], sib_send.at[it], sib_recv.at[it], sibling)
        if it == 0:
            wait_for(costbuf.at[pl.ds(0, PLANE - 1)], cost_recv)
            costbuf[20] = costrow[...]
            cost_total = jnp.sum(jnp.sum(costbuf[...], axis=0), axis=1, keepdims=True)
        wait_for(sib.at[it], sib_recv.at[it])
        if it == 0:
            dem_total = jnp.sum(dem4 + sib[it, 2 * COLB:2 * COLB + 1, :], axis=1, keepdims=True)
            omega = jnp.sqrt(cost_total) / jnp.sqrt(dem_total)
            tau = step_s[0] / omega
            sigma = step_s[0] * omega
        was = primal[...] if it == 0 else xcur[...]
        back = dense[it, 0:2 * COLB, :] + sib[it, 0:2 * COLB, :]
        now = jnp.maximum(0.0, was - tau * (cost[...] - back))
        xbar[...] = 2.0 * now - was
        if it == ITERS - 1:
            primal_o[...] = now
            put_primal = fetch(primal_o, primal_oh, out_sem.at[0])
        else:
            xcur[...] = now

        products(SLOTS, UNROLL, xbar, lambda s: 2 * bcol_s[s], blk, prodf, True)
        put_pairs(part.at[it], scatter(row_hot, prodf[...]))

        def send_chunk(j, it=it):
            ty, tz = plane_peer(j)
            at = pl.multiple_of((lax.rem(ty, 2) * 4 + lax.rem(tz, 4)) * CHUNK, CHUNK)
            send(part.at[it, pl.ds(at, CHUNK)], rsbuf.at[it, j], rs_send.at[it], rs_recv.at[it],
                 (r, ty * ZN + tz))

        each_plane(send_chunk)
        rsbuf[it, 20] = part[it, pl.ds(my_at, CHUNK), :]
        wait_for(rsbuf.at[it, pl.ds(0, PLANE - 1)], rs_recv.at[it])
        fore = jnp.sum(rsbuf[it], axis=0)
        y_was = dual[pl.ds(my_at, CHUNK), :] if it == 0 else ybuf[it - 1, pl.ds(my_at, CHUNK), :]
        y_now = jnp.maximum(0.0, y_was + sigma * (demand[pl.ds(my_at, CHUNK), :] - fore))
        held = ybuf.at[it] if it < ITERS - 1 else yall.at[core, x]
        held[pl.ds(my_at, CHUNK), :] = y_now
        chunk = held.at[pl.ds(my_at, CHUNK)]

        def send_dual(dx, k, it=it, chunk=chunk):
            ty = lax.rem(y + k // 4, YN)
            tz = lax.rem(z + lax.rem(k, 4) + ZN - 1, ZN)
            send(chunk, chunk, ag_send.at[it], ag_recv.at[it],
                 (lax.rem(x + dx, XN) * 2 + core, ty * ZN + tz))
            return 0

        if it == ITERS - 1:
            lax.fori_loop(0, 3 * 8, lambda m, _: send_dual(lax.rem(m // 8 + 1, 3) + 1, lax.rem(m, 8)), 0)
        lax.fori_loop(2, 8, lambda k, _: send_dual(0, k), 0)
        send_dual(0, 0)
        if it < ITERS - 1:
            wait_for(held.at[pl.ds(0, 7 * CHUNK)], ag_recv.at[it])
            back_products(held, prod.at[it + 1])

    new_hot = (lax.broadcasted_iota(jnp.int32, (NEW, NEW), 0) == fcol_v[...]).astype(F32).astype(BF)
    fresh_copy.wait()
    wait_for(rsbuf.at[0, pl.ds(0, PLANE - 1)], ag_recv.at[ITERS - 1])
    send(yall.at[core], yall.at[core], fs_send, fs_recv, sibling)
    dual_o[...] = yall[core, x]
    put_dual = fetch(dual_o, dual_oh, out_sem.at[1])
    wait_for(yall.at[core], fs_recv)

    yflat = yall.reshape(2 * XN * 2 * ROWB, LANES)

    def new_at(s):
        block = frow_s[s]
        rr = block // ROWB
        return lax.rem(rr, 2) * (XN * 2 * ROWB) + (rr // 2) * (2 * ROWB) + lax.rem(block, ROWB) * 2

    products(NEW, UNROLL_NEW, yflat, new_at, frs, prodn, False)
    put_pairs(priced, scatter(new_hot, prodn[...]))
    reduced_o[...] = fcost[...] - priced[...]
    put_reduced = fetch(reduced_o, reduced_oh, out_sem.at[2])

    put_primal.wait()
    put_dual.wait()
    put_reduced.wait()
    wait_for(yall.at[core], fs_send)
    wait_for(metabuf, meta_send)
    wait_for(costbuf.at[pl.ds(0, PLANE - 1)], cost_send)
    for it in range(ITERS):
        wait_for(pbuf.at[it], px_send.at[it])
        wait_for(sib.at[it], sib_send.at[it])
        wait_for(rsbuf.at[it, pl.ds(0, PLANE - 1)], rs_send.at[it])
        wait_for(rsbuf.at[it, pl.ds(0, 7 if it < ITERS - 1 else PLANE - 1)], ag_send.at[it])


def local(
    blocks, block_row, block_col, block_count, primal, dual, cost, demand, step,
    fresh_pattern_blocks, fresh_block_row, fresh_block_column, fresh_pattern_cost,
):
    hbm = pl.BlockSpec(memory_space=pltpu.HBM)
    dma = pltpu.SemaphoreType.DMA
    smem_i = lambda n: pltpu.SMEM((n,), jnp.int32)
    vec_i = lambda n: pltpu.VMEM((1, n), jnp.int32)
    f32 = lambda *shape: pltpu.VMEM(shape, F32)
    rows2 = lambda v: v.reshape(-1, LANES)
    outs = pl.pallas_call(
        kernel,
        out_shape=(
            jax.ShapeDtypeStruct((2 * COLB, LANES), F32),
            jax.ShapeDtypeStruct((2 * ROWB, LANES), F32),
            jax.ShapeDtypeStruct((2 * NEW, LANES), F32),
        ),
        in_specs=[hbm] * 15,
        out_specs=(hbm, hbm, hbm),
        scratch_shapes=[
            f32(2 * COLB, LANES), f32(2 * ROWB, LANES), f32(2 * NEW, LANES), dma((3,)),
            smem_i(SLOTS), smem_i(SLOTS), smem_i(1), smem_i(NEW), pltpu.SMEM((1,), F32),
            vec_i(SLOTS), vec_i(SLOTS), vec_i(NEW),
            f32(2 * COLB, LANES), f32(2 * ROWB, LANES), f32(2 * COLB, LANES), f32(2 * ROWB, LANES),
            f32(2 * NEW, LANES),
            pltpu.VMEM((SLOTS, EDGE, EDGE), BF),
            pltpu.VMEM((NEW, EDGE, EDGE), BF),
            f32(ITERS, SLOTS, EDGE), f32(ITERS, XN - 1, SLOTS, EDGE),
            f32(8, LANES), f32(XN - 1, 8, LANES),
            f32(ITERS, 2 * COLB + 8, LANES), f32(ITERS, 2 * COLB + 8, LANES),
            f32(1, LANES), f32(PLANE, 1, LANES),
            f32(2 * COLB, LANES), f32(2 * COLB, LANES), f32(SLOTS, EDGE),
            f32(ITERS, 2 * ROWB, LANES), f32(ITERS, PLANE, CHUNK, LANES),
            f32(ITERS, 2 * ROWB, LANES), f32(2, XN, 2 * ROWB, LANES),
            f32(NEW, EDGE), f32(2 * NEW, LANES),
            dma((13,)), dma((LOADS,)), dma,
            dma((ITERS,)), dma((ITERS, XN - 1)), dma, dma, dma, dma,
            dma((ITERS,)), dma((ITERS,)), dma((ITERS,)), dma((ITERS,)),
            dma((ITERS,)), dma((ITERS,)), dma, dma,
        ],
        compiler_params=pltpu.CompilerParams(
            collective_id=0, has_side_effects=True, vmem_limit_bytes=60 * 2**20
        ),
    )(
        block_row, block_col, block_count, fresh_block_row, step,
        block_col.reshape(1, -1), block_row.reshape(1, -1), fresh_block_column.reshape(1, -1),
        rows2(primal), rows2(dual), rows2(cost), rows2(demand), rows2(fresh_pattern_cost),
        blocks, fresh_pattern_blocks,
    )
    def hand_over(*refs):
        sems = refs[-1]
        ins = [fetch(refs[i], refs[i + 6], sems.at[i]) for i in range(3)]
        copies = []
        for i in (0, 1, 2):
            ins[i].wait()
            copies.append(fetch(refs[i + 6], refs[i + 3], sems.at[i + 3]))
        for copy in copies:
            copy.wait()

    outs = pl.pallas_call(
        hand_over,
        out_shape=tuple(jax.ShapeDtypeStruct(o.shape, F32) for o in outs),
        in_specs=[hbm] * 3,
        out_specs=(hbm, hbm, hbm),
        scratch_shapes=[pltpu.VMEM(o.shape, F32) for o in outs] + [dma((6,))],
        compiler_params=pltpu.CompilerParams(vmem_limit_bytes=60 * 2**20),
    )(*outs)
    return tuple(o.reshape(-1) for o in outs)


def solution(mesh):
    both = ("rows", "cols")
    placed = (
        P(both, None, None), P(both), P(both), P(both),
        P("cols"), P("rows"), P("cols"), P("rows"), P(),
        P(both, None, None), P(both), P(both), P(both),
    )
    return jax.shard_map(
        local, mesh=mesh, in_specs=placed,
        out_specs=(P("cols"), P("rows"), P(both)), check_vma=False,
    )
```

time: 76.9 us -> 60.2 us (0.78)
  local copies, waits for them, and re-layouts: 13.6 us -> 0 us
  Pallas kernels: 60.9 us -> 58.1 us
    unnamed x25 -> x0, local copies, waits for them, and re-layouts: 13.6 us -> none
    pallas_call x1, Pallas kernels: 60.9 us -> 56.5 us  [local(): pl.pallas_call(kernel, out_shape=(jax.ShapeDtypeStruct((2 * COLB, LANES),...]
    pallas_call x0 -> x1, Pallas kernels: none -> 1.63 us  [local(): pl.pallas_call(hand_over, out_shape=tuple((jax.ShapeDtypeStruct(o.shape,...]
where the time goes in v2:
time: 60.2 us; the launch traced here: 60 us
  Pallas kernels  58.1 us (97%)
  between operations  1.93 us (3%)
    pallas_call x1, Pallas kernels, local(): pl.pallas_call(kernel, out_shape=(jax.ShapeDtypeStruct((2 * COLB, LANES),...  56.5 us
    pallas_call x1, Pallas kernels, local(): pl.pallas_call(hand_over, out_shape=tuple((jax.ShapeDtypeStruct(o.shape,...  1.63 us

profile of v2, /device:TPU:1, one launch (start us, length us, event | category | flops | bytes accessed | tf_op | source)
XLA Modules:
  0.0 60.0 jit_solution(8402783861216785405)
XLA Ops:
  1.9 56.5 %shard_map.148 = (f32[256,128]{1,0:T(8,128)}, f32[64,128]{1,0:T(8,128)}, f32[64,128]{1,0:T(8,128)}) custom-call(s32[48]{0:T(128)} %brow_h.1, s32[48]{0:T(128)} %bcol_h.1, s32[1]{0:T(128)S(6)} %copy.16.cnt_h, s32[32]{0:T(128)} %frow_h.1, f32[1]{0:T(128)S(6)} %copy.17.step_h, s32[1,48]{1,0:T(1,128)} %bitcast.17, s32[1,48]{1,0:T(1,128)} %bitcast.16, ...), custom_call_target="tpu_custom_call" | custom-call | tf_op jit(solution)/shard_map/pallas_call | solution.py:297
  58.4 1.6 %shard_map.149 = (f32[256,128]{1,0:T(8,128)}, f32[64,128]{1,0:T(8,128)}, f32[64,128]{1,0:T(8,128)}) custom-call(f32[256,128]{1,0:T(8,128)} %get-tuple-element.9.refs_0_, f32[64,128]{1,0:T(8,128)} %get-tuple-element.10.refs_1_, f32[64,128]{1,0:T(8,128)} %get-tuple-element.11.refs_2_), custom_call_target="tpu_custom_call" | custom-call | tf_op jit(solution)/shard_map/pallas_call | solution.py:346

commit v3 on v2

v3 whole, which is shorter than its diff:
```python
import jax
import jax.numpy as jnp
from jax import lax
from jax.sharding import PartitionSpec as P
from jax.experimental import pallas as pl
from jax.experimental.pallas import tpu as pltpu

MESH = pl.DeviceIdType.MESH
ITERS = 2
EDGE = 256
LANES = 128
SLOTS = 48
HALF = SLOTS // 2
NEW = 32
XN, YN, ZN = 4, 4, 8
PLANE = YN * ZN
COLB = 128
ROWB = 32
CHUNK = 8
PAD = 64
BF = jnp.bfloat16
F32 = jnp.float32
LOADS = 4
UNROLL = 24
UNROLL_NEW = 16
UNROLL_T = 4


def hops(p):
    ring = lambda d, n: min(d % n, -d % n)
    return ring(p[0], XN) + ring(p[1], YN) + ring(p[2], ZN)


def far_first(peers):
    return sorted([p for p in peers if hops(p)], key=lambda p: -hops(p))


PLANE_PEERS = far_first([(0, dy, dz) for dy in range(YN) for dz in range(ZN)])
NEAR = [(0, dy, dz) for dy in (0, 1) for dz in (-1, 0, 1, 2)]
NEAR_PEERS = far_first(NEAR)
LAST_PEERS = far_first([(dx, dy, dz) for dx in range(XN) for _, dy, dz in NEAR])
X_PEERS = (2, 1, 3)


def split3(v):
    hi = v.astype(BF).astype(F32)
    rest = v - hi
    mid = rest.astype(BF).astype(F32)
    return hi, mid, rest - mid


def piece_tile(ref, at, lane_row):
    v = jnp.concatenate([ref[pl.ds(at, 1), :], ref[pl.ds(at + 1, 1), :]], axis=1)
    v = jnp.broadcast_to(v, (8, EDGE))
    hi, mid, lo = split3(v)
    tile = jnp.where(lane_row == 0, hi, jnp.where(lane_row == 1, mid, lo))
    return jnp.where(lane_row < 3, tile, 0.0).astype(BF)


def put_tiles(ref, val):
    n = val.shape[0]
    for k, part in enumerate(split3(val)):
        for h in range(2):
            ref[h, pl.ds(k, n, stride=8), :] = part[:, h * LANES:(h + 1) * LANES]


def pairs(ref, n):
    return jnp.concatenate([ref[pl.ds(0, n, stride=2), :], ref[pl.ds(1, n, stride=2), :]], axis=1)


def put_pairs(ref, val):
    n = val.shape[0]
    ref[pl.ds(0, n, stride=2), :] = val[:, :LANES]
    ref[pl.ds(1, n, stride=2), :] = val[:, LANES:]


def products(first, count, unroll, tile_of, blk_ref, out_ref):
    def step(i, _):
        for u in range(unroll):
            s = first + i * unroll + u
            res = jnp.dot(tile_of(s), blk_ref[s], preferred_element_type=F32)
            for h in range(2):
                out_ref[h, pl.ds(pl.multiple_of(s * 8, 8), 8), :] = res[:, h * LANES:(h + 1) * LANES]
        return 0

    if count == unroll:
        step(0, 0)
    else:
        lax.fori_loop(0, count // unroll, step, 0)


def summed(ref, first, count):
    def half(h):
        parts = [ref[h, pl.ds(first * 8 + k, count, stride=8), :] for k in range(3)]
        return parts[0] + parts[1] + parts[2]

    return jnp.concatenate([half(0), half(1)], axis=1)


def hot3(ids, row):
    lane = lax.broadcasted_iota(jnp.int32, (1, LANES), 1)
    third = jnp.where(lane < PAD, row, -1.0)
    n = ids.shape[0]
    hot = [(ids == jnp.broadcast_to(v, (n, LANES))).astype(F32).astype(BF) for v in (row, third)]
    return jnp.concatenate(hot, axis=1)


def scatter(hot, prod):
    n = prod.shape[0]
    zeros = jnp.zeros((PAD - n, EDGE), BF)
    rows = []
    for part in split3(prod):
        rows += [part.astype(BF), zeros]
    rows.append(jnp.zeros((PAD, EDGE), BF))
    return jnp.dot(hot, jnp.concatenate(rows, axis=0), preferred_element_type=F32)


def send(src, dst, send_sem, recv_sem, device):
    pltpu.make_async_remote_copy(
        src_ref=src, dst_ref=dst, send_sem=send_sem, recv_sem=recv_sem,
        device_id=device, device_id_type=MESH,
    ).start()


def wait_for(ref, sem):
    pltpu.make_async_copy(ref, ref, sem).wait()


def fetch(src, dst, sem):
    copy = pltpu.make_async_copy(src, dst, sem)
    copy.start()
    return copy


def kernel(
    brow_h, bcol_h, cnt_h, frow_h, step_h, bcolv_h, browv_h, fcolv_h,
    primal_h, dual_h, cost_h, demand_h, fcost_h, blocks, fresh,
    primal_oh, dual_oh, reduced_oh,
    primal_o, dual_o, reduced_o, out_sem,
    brow_s, bcol_s, cnt_s, frow_s, step_s, bcol_v, brow_v, fcol_v,
    primal, dual, cost, demand, fcost, rows,
    blk, blk_t, frs, prod, pbuf, meta, metabuf, dense, sib, demrow, costrow, costbuf,
    xcur, price, xtile, ytile, prod8, part, rsbuf, ybuf, yall, priced,
    in_sem, load_sem, fresh_sem, px_send, px_recv, meta_send, meta_recv, cost_send, cost_recv,
    dem_send, dem_recv, sib_send, sib_recv, rs_send, rs_recv, ag_send, ag_recv, fs_send, fs_recv,
):
    r = lax.axis_index("rows")
    c = lax.axis_index("cols")
    x, core = r // 2, lax.rem(r, 2)
    y, z = c // ZN, lax.rem(c, ZN)
    per = SLOTS // LOADS

    first = [
        fetch(src, dst, in_sem.at[i])
        for i, (src, dst) in enumerate([(brow_h, brow_s), (dual_h, dual)])
    ]
    loads = [
        fetch(blocks.at[pl.ds(i * per, per)], blk.at[pl.ds(i * per, per)], load_sem.at[i])
        for i in range(LOADS)
    ]
    inputs = [
        (cnt_h, cnt_s), (bcolv_h, bcol_v), (browv_h, brow_v), (cost_h, cost), (demand_h, demand),
        (step_h, step_s), (bcol_h, bcol_s), (primal_h, primal),
        (frow_h, frow_s), (fcolv_h, fcol_v), (fcost_h, fcost),
    ]
    rest = [fetch(src, dst, in_sem.at[i + 2]) for i, (src, dst) in enumerate(inputs)]

    def at_offset(p):
        dx, dy, dz = p
        return (
            lax.rem(x + dx, XN) * 2 + core if dx else r,
            lax.rem(y + dy, YN) * ZN + lax.rem(z + dz + ZN, ZN),
        )

    sibling = (x * 2 + 1 - core, c)
    x_peers = [at_offset((d, 0, 0)) for d in X_PEERS]
    barrier = pltpu.get_barrier_semaphore()

    def greet(device):
        pl.semaphore_signal(barrier, inc=1, device_id=device, device_id_type=MESH)

    for p in PLANE_PEERS:
        greet(at_offset(p))
    for device in x_peers:
        greet(device)
    greet(sibling)

    xtile[...] = jnp.zeros_like(xtile)
    ytile[...] = jnp.zeros_like(ytile)

    for copy in first + rest:
        copy.wait()
    put_tiles(ytile, pairs(dual, ROWB))
    lane = lax.broadcasted_iota(jnp.int32, (1, LANES), 1)
    alive = lane < cnt_s[0]
    rows[...] = jnp.full((8, LANES), -1, jnp.int32)
    rows[0:1, 0:SLOTS] = bcol_v[...]
    rows[1:2, 0:SLOTS] = brow_v[...]
    rows[2:3, 0:NEW] = fcol_v[...]

    def twice(row, keep):
        kept = jnp.where(keep, row, -1).astype(F32)
        return jnp.where(lane < PAD, kept, pltpu.roll(kept, PAD, 1))

    my_cols = twice(rows[0:1, :], alive)
    my_rows = twice(rows[1:2, :], alive)
    new_cols = twice(rows[2:3, :], lane < NEW)
    row_ids = lax.broadcasted_iota(jnp.int32, (ROWB, LANES), 0).astype(F32)
    col_ids = lax.broadcasted_iota(jnp.int32, (COLB, LANES), 0).astype(F32)

    dem_sq = jnp.sum(demand[...] * demand[...], axis=0, keepdims=True)
    meta[...] = jnp.zeros_like(meta)
    meta[0:1, :] = my_cols
    meta[1:2, :] = dem_sq
    costrow[...] = jnp.sum(cost[...] * cost[...], axis=0, keepdims=True)
    price[...] = pairs(cost, COLB)
    xcur[...] = pairs(primal, COLB)

    def block_tile(ref, ids):
        tiles = ref.reshape(2, ref.shape[1] // 8, 8, LANES)

        def tile(s):
            at = ids[s]
            return jnp.concatenate([tiles[0, at], tiles[1, at]], axis=1).astype(BF)

        return tile

    my_chunk = lax.rem(y, 2) * 4 + lax.rem(z, 4)
    my_at = pl.multiple_of(my_chunk * CHUNK, CHUNK)
    tau = sigma = None
    fresh_copy = None
    for it in range(ITERS):
        for h in range(2):
            if it == 0:
                for copy in loads[h * LOADS // 2:(h + 1) * LOADS // 2]:
                    copy.wait()
            products(h * HALF, HALF, UNROLL, block_tile(ytile, brow_s), blk, prod8)
            half = pl.ds(h * HALF, HALF)
            prod[it, half, :] = summed(prod8, h * HALF, HALF)
            if it == 0 and h == 0:
                continue
            if it == 0:
                fresh_copy = fetch(fresh, frs, fresh_sem)
                pl.semaphore_wait(barrier, len(PLANE_PEERS) + len(X_PEERS) + 1)
                for d, device in enumerate(x_peers):
                    send(meta, metabuf.at[d], meta_send, meta_recv, device)
                half = pl.ds(0, SLOTS)
            for d, device in enumerate(x_peers):
                send(prod.at[it, half], pbuf.at[it, d, half], px_send.at[it], px_recv.at[it, d], device)
        if it == 0:
            for j, p in enumerate(PLANE_PEERS):
                send(costrow, costbuf.at[j], cost_send, cost_recv, at_offset(p))

            def turn(i, _):
                for u in range(UNROLL_T):
                    s = i * UNROLL_T + u
                    blk_t[s] = blk[s].T
                return 0

            lax.fori_loop(0, SLOTS // UNROLL_T, turn, 0)
        total = scatter(hot3(col_ids, my_cols), prod[it])
        if it == 0:
            wait_for(metabuf, meta_recv)
        for d in (1, 2, 0):
            wait_for(pbuf.at[it, d], px_recv.at[it, d])
            total = total + scatter(hot3(col_ids, metabuf[d, 0:1, :]), pbuf[it, d])
        dense[it] = total
        send(dense.at[it], sib.at[it], sib_send.at[it], sib_recv.at[it], sibling)
        if it == 0:
            dem4 = dem_sq + metabuf[0, 1:2, :] + metabuf[1, 1:2, :] + metabuf[2, 1:2, :]
            demrow[0] = dem4
            send(demrow.at[0], demrow.at[1], dem_send, dem_recv, sibling)
            wait_for(costbuf, cost_recv)
            cost_all = jnp.sum(costbuf[...], axis=0) + costrow[...]
            cost_total = jnp.sum(cost_all, axis=1, keepdims=True)
            wait_for(demrow.at[1], dem_recv)
            dem_total = jnp.sum(dem4 + demrow[1], axis=1, keepdims=True)
            omega = jnp.sqrt(cost_total) / jnp.sqrt(dem_total)
            tau = step_s[0] / omega
            sigma = step_s[0] * omega
        was = xcur[...]
        wait_for(sib.at[it], sib_recv.at[it])
        now = jnp.maximum(0.0, was - tau * (price[...] - (dense[it] + sib[it])))
        put_tiles(xtile, 2.0 * now - was)
        xcur[...] = now

        products(0, SLOTS, UNROLL, block_tile(xtile, bcol_s), blk_t, prod8)
        put_pairs(part.at[it], scatter(hot3(row_ids, my_rows), summed(prod8, 0, SLOTS)))
        for j, p in enumerate(PLANE_PEERS):
            target = at_offset(p)
            ty, tz = target[1] // ZN, lax.rem(target[1], ZN)
            at = pl.multiple_of((lax.rem(ty, 2) * 4 + lax.rem(tz, 4)) * CHUNK, CHUNK)
            send(part.at[it, pl.ds(at, CHUNK)], rsbuf.at[it, j], rs_send.at[it], rs_recv.at[it], target)
        if it == ITERS - 1:
            put_pairs(primal_o, xcur[...])
            put_primal = fetch(primal_o, primal_oh, out_sem.at[0])
        y_was = dual[pl.ds(my_at, CHUNK), :] if it == 0 else ybuf[it - 1, pl.ds(my_at, CHUNK), :]
        mine = part[it, pl.ds(my_at, CHUNK), :]
        wait_for(rsbuf.at[it], rs_recv.at[it])
        fore = mine + jnp.sum(rsbuf[it], axis=0)
        y_now = jnp.maximum(0.0, y_was + sigma * (demand[pl.ds(my_at, CHUNK), :] - fore))
        held = ybuf.at[it] if it < ITERS - 1 else yall.at[core, x]
        held[pl.ds(my_at, CHUNK), :] = y_now
        chunk = held.at[pl.ds(my_at, CHUNK)]
        for p in NEAR_PEERS if it < ITERS - 1 else LAST_PEERS:
            send(chunk, chunk, ag_send.at[it], ag_recv.at[it], at_offset(p))
        if it < ITERS - 1:
            wait_for(held.at[pl.ds(0, len(NEAR_PEERS) * CHUNK)], ag_recv.at[it])
            put_tiles(ytile, pairs(held, ROWB))

    new_hot = hot3(row_ids, new_cols)
    lane_row = lax.broadcasted_iota(jnp.int32, (8, EDGE), 0)
    fresh_copy.wait()
    wait_for(rsbuf.at[0], ag_recv.at[ITERS - 1])
    send(yall.at[core], yall.at[core], fs_send, fs_recv, sibling)
    dual_o[...] = yall[core, x]
    put_dual = fetch(dual_o, dual_oh, out_sem.at[1])
    wait_for(yall.at[core], fs_recv)

    yflat = yall.reshape(2 * XN * 2 * ROWB, LANES)

    def new_tile(s):
        block = frow_s[s]
        rr = block // ROWB
        at = lax.rem(rr, 2) * (XN * 2 * ROWB) + (rr // 2) * (2 * ROWB) + lax.rem(block, ROWB) * 2
        return piece_tile(yflat, at, lane_row)

    products(0, NEW, UNROLL_NEW, new_tile, frs, prod8)
    put_pairs(priced, scatter(new_hot, summed(prod8, 0, NEW)))
    reduced_o[...] = fcost[...] - priced[...]
    put_reduced = fetch(reduced_o, reduced_oh, out_sem.at[2])

    wait_for(yall.at[core], fs_send)
    wait_for(metabuf, meta_send)
    wait_for(costbuf, cost_send)
    wait_for(demrow.at[1], dem_send)
    for it in range(ITERS):
        wait_for(pbuf.at[it], px_send.at[it])
        wait_for(sib.at[it], sib_send.at[it])
        wait_for(rsbuf.at[it], rs_send.at[it])
        wait_for(rsbuf.at[it, pl.ds(0, len(NEAR_PEERS if it < ITERS - 1 else LAST_PEERS))], ag_send.at[it])
    put_primal.wait()
    put_dual.wait()
    put_reduced.wait()


def hand_over(*refs):
    sems = refs[-1]
    ins = [fetch(refs[i], refs[i + 6], sems.at[i]) for i in range(3)]
    outs = []
    for i in range(3):
        ins[i].wait()
        outs.append(fetch(refs[i + 6], refs[i + 3], sems.at[i + 3]))
    for copy in outs:
        copy.wait()


def local(
    blocks, block_row, block_col, block_count, primal, dual, cost, demand, step,
    fresh_pattern_blocks, fresh_block_row, fresh_block_column, fresh_pattern_cost,
):
    hbm = pl.BlockSpec(memory_space=pltpu.HBM)
    dma = pltpu.SemaphoreType.DMA
    smem_i = lambda n: pltpu.SMEM((n,), jnp.int32)
    vec_i = lambda n: pltpu.VMEM((1, n), jnp.int32)
    f32 = lambda *shape: pltpu.VMEM(shape, F32)
    rows2 = lambda v: v.reshape(-1, LANES)
    out_rows = (2 * COLB, 2 * ROWB, 2 * NEW)
    outs = pl.pallas_call(
        kernel,
        out_shape=tuple(jax.ShapeDtypeStruct((n, LANES), F32) for n in out_rows),
        in_specs=[hbm] * 15,
        out_specs=(hbm, hbm, hbm),
        scratch_shapes=[
            *[f32(n, LANES) for n in out_rows], dma((3,)),
            smem_i(SLOTS), smem_i(SLOTS), smem_i(1), smem_i(NEW), pltpu.SMEM((1,), F32),
            vec_i(SLOTS), vec_i(SLOTS), vec_i(NEW),
            f32(2 * COLB, LANES), f32(2 * ROWB, LANES), f32(2 * COLB, LANES), f32(2 * ROWB, LANES),
            f32(2 * NEW, LANES), pltpu.VMEM((8, LANES), jnp.int32),
            pltpu.VMEM((SLOTS, EDGE, EDGE), BF),
            pltpu.VMEM((SLOTS, EDGE, EDGE), BF),
            pltpu.VMEM((NEW, EDGE, EDGE), BF),
            f32(ITERS, SLOTS, EDGE), f32(ITERS, XN - 1, SLOTS, EDGE),
            f32(8, LANES), f32(XN - 1, 8, LANES),
            f32(ITERS, COLB, EDGE), f32(ITERS, COLB, EDGE),
            f32(2, 1, LANES), f32(1, LANES), f32(PLANE - 1, 1, LANES),
            f32(COLB, EDGE), f32(COLB, EDGE), f32(2, 8 * COLB, LANES), f32(2, 8 * ROWB, LANES),
            f32(2, 8 * SLOTS, LANES),
            f32(ITERS, 2 * ROWB, LANES), f32(ITERS, PLANE - 1, CHUNK, LANES),
            f32(ITERS, 2 * ROWB, LANES), f32(2, XN, 2 * ROWB, LANES),
            f32(2 * NEW, LANES),
            dma((13,)), dma((LOADS,)), dma,
            dma((ITERS,)), dma((ITERS, XN - 1)), dma, dma, dma, dma, dma, dma,
            dma((ITERS,)), dma((ITERS,)), dma((ITERS,)), dma((ITERS,)),
            dma((ITERS,)), dma((ITERS,)), dma, dma,
        ],
        compiler_params=pltpu.CompilerParams(
            collective_id=0, has_side_effects=True, vmem_limit_bytes=60 * 2**20
        ),
    )(
        block_row, block_col, block_count, fresh_block_row, step,
        block_col.reshape(1, -1), block_row.reshape(1, -1), fresh_block_column.reshape(1, -1),
        rows2(primal), rows2(dual), rows2(cost), rows2(demand), rows2(fresh_pattern_cost),
        blocks, fresh_pattern_blocks,
    )
    outs = pl.pallas_call(
        hand_over,
        out_shape=tuple(jax.ShapeDtypeStruct(o.shape, F32) for o in outs),
        in_specs=[hbm] * 3,
        out_specs=(hbm, hbm, hbm),
        scratch_shapes=[f32(n, LANES) for n in out_rows] + [dma((6,))],
        compiler_params=pltpu.CompilerParams(vmem_limit_bytes=60 * 2**20),
    )(*outs)
    return tuple(o.reshape(-1) for o in outs)


def solution(mesh):
    both = ("rows", "cols")
    placed = (
        P(both, None, None), P(both), P(both), P(both),
        P("cols"), P("rows"), P("cols"), P("rows"), P(),
        P(both, None, None), P(both), P(both), P(both),
    )
    return jax.shard_map(
        local, mesh=mesh, in_specs=placed,
        out_specs=(P("cols"), P("rows"), P(both)), check_vma=False,
    )
```

time: 60.2 us -> 56.2 us (0.934)
  Pallas kernels: 58.1 us -> 54.1 us
    pallas_call x1, Pallas kernels: 56.5 us -> 52.5 us  [local(): pl.pallas_call(kernel, out_shape=tuple((jax.ShapeDtypeStruct((n, LANES),...]
where the time goes in v3:
time: 56.2 us; the launch traced here: 56.1 us
  Pallas kernels  54.1 us (96%)
  between operations  1.93 us (3%)
    pallas_call x1, Pallas kernels, local(): pl.pallas_call(kernel, out_shape=tuple((jax.ShapeDtypeStruct((n, LANES),...  52.5 us
    pallas_call x1, Pallas kernels, local(): pl.pallas_call(hand_over, out_shape=tuple((jax.ShapeDtypeStruct(o.shape,...  1.63 us

profile of v3, /device:TPU:1, one launch (start us, length us, event | category | flops | bytes accessed | tf_op | source)
XLA Modules:
  0.0 56.1 jit_solution(18147609815069805403)
XLA Ops:
  1.9 52.5 %shard_map.148 = (f32[256,128]{1,0:T(8,128)}, f32[64,128]{1,0:T(8,128)}, f32[64,128]{1,0:T(8,128)}) custom-call(s32[48]{0:T(128)} %brow_h.1, s32[48]{0:T(128)} %bcol_h.1, s32[1]{0:T(128)S(6)} %copy.16.cnt_h, s32[32]{0:T(128)} %frow_h.1, f32[1]{0:T(128)S(6)} %copy.17.step_h, s32[1,48]{1,0:T(1,128)} %bitcast.17, s32[1,48]{1,0:T(1,128)} %bitcast.16, ...), custom_call_target="tpu_custom_call" | custom-call | tf_op jit(solution)/shard_map/pallas_call | solution.py:369
  54.4 1.6 %shard_map.149 = (f32[256,128]{1,0:T(8,128)}, f32[64,128]{1,0:T(8,128)}, f32[64,128]{1,0:T(8,128)}) custom-call(f32[256,128]{1,0:T(8,128)} %get-tuple-element.9.refs_0_, f32[64,128]{1,0:T(8,128)} %get-tuple-element.10.refs_1_, f32[64,128]{1,0:T(8,128)} %get-tuple-element.11.refs_2_), custom_call_target="tpu_custom_call" | custom-call | tf_op jit(solution)/shard_map/pallas_call | solution.py:406

commit v4 on v3

--- a/solution.py
+++ b/solution.py
@@ -21,8 +21,8 @@
 BF = jnp.bfloat16
 F32 = jnp.float32
 LOADS = 4
-UNROLL = 24
-UNROLL_NEW = 16
+UNROLL = 48
+UNROLL_NEW = 32
 UNROLL_T = 4
 
 
@@ -140,7 +140,7 @@
     brow_s, bcol_s, cnt_s, frow_s, step_s, bcol_v, brow_v, fcol_v,
     primal, dual, cost, demand, fcost, rows,
     blk, blk_t, frs, prod, pbuf, meta, metabuf, dense, sib, demrow, costrow, costbuf,
-    xcur, price, xtile, ytile, prod8, part, rsbuf, ybuf, yall, priced,
+    xcur, price, xtile, ytile, prod8, part, rsbuf, ybuf, yall, priced, hots, row_hot, new_hot,
     in_sem, load_sem, fresh_sem, px_send, px_recv, meta_send, meta_recv, cost_send, cost_recv,
     dem_send, dem_recv, sib_send, sib_recv, rs_send, rs_recv, ag_send, ag_recv, fs_send, fs_recv,
 ):
@@ -149,6 +149,27 @@
     x, core = r // 2, lax.rem(r, 2)
     y, z = c // ZN, lax.rem(c, ZN)
     per = SLOTS // LOADS
+
+    def at_offset(p):
+        dx, dy, dz = p
+        return (
+            lax.rem(x + dx, XN) * 2 + core if dx else r,
+            lax.rem(y + dy, YN) * ZN + lax.rem(z + dz + ZN, ZN),
+        )
+
+    sibling = (x * 2 + 1 - core, c)
+    x_peers = [at_offset((d, 0, 0)) for d in X_PEERS]
+    barrier = pltpu.get_barrier_semaphore()
+
+    def greet(device):
+        pl.semaphore_signal(barrier, inc=1, device_id=device, device_id_type=MESH)
+
+    plane = [at_offset(p) for p in PLANE_PEERS]
+    for device in plane:
+        greet(device)
+    for device in x_peers:
+        greet(device)
+    greet(sibling)
 
     first = [
         fetch(src, dst, in_sem.at[i])
@@ -165,26 +186,6 @@
     ]
     rest = [fetch(src, dst, in_sem.at[i + 2]) for i, (src, dst) in enumerate(inputs)]
 
-    def at_offset(p):
-        dx, dy, dz = p
-        return (
-            lax.rem(x + dx, XN) * 2 + core if dx else r,
-            lax.rem(y + dy, YN) * ZN + lax.rem(z + dz + ZN, ZN),
-        )
-
-    sibling = (x * 2 + 1 - core, c)
-    x_peers = [at_offset((d, 0, 0)) for d in X_PEERS]
-    barrier = pltpu.get_barrier_semaphore()
-
-    def greet(device):
-        pl.semaphore_signal(barrier, inc=1, device_id=device, device_id_type=MESH)
-
-    for p in PLANE_PEERS:
-        greet(at_offset(p))
-    for device in x_peers:
-        greet(device)
-    greet(sibling)
-
     xtile[...] = jnp.zeros_like(xtile)
     ytile[...] = jnp.zeros_like(ytile)
 
@@ -227,6 +228,14 @@
 
     my_chunk = lax.rem(y, 2) * 4 + lax.rem(z, 4)
     my_at = pl.multiple_of(my_chunk * CHUNK, CHUNK)
+    chunk_at = [
+        pl.multiple_of((lax.rem(y + dy, 2) * 4 + lax.rem(z + dz, 4)) * CHUNK, CHUNK)
+        for _, dy, dz in PLANE_PEERS
+    ]
+    near = [at_offset(p) for p in NEAR_PEERS]
+    last = [at_offset(p) for p in LAST_PEERS]
+    pending = []
+    left = lambda ref, sem: pending.append(lambda: wait_for(ref, sem))
     tau = sigma = None
     fresh_copy = None
     for it in range(ITERS):
@@ -234,7 +243,7 @@
             if it == 0:
                 for copy in loads[h * LOADS // 2:(h + 1) * LOADS // 2]:
                     copy.wait()
-            products(h * HALF, HALF, UNROLL, block_tile(ytile, brow_s), blk, prod8)
+            products(h * HALF, HALF, HALF, block_tile(ytile, brow_s), blk, prod8)
             half = pl.ds(h * HALF, HALF)
             prod[it, half, :] = summed(prod8, h * HALF, HALF)
             if it == 0 and h == 0:
@@ -244,12 +253,15 @@
                 pl.semaphore_wait(barrier, len(PLANE_PEERS) + len(X_PEERS) + 1)
                 for d, device in enumerate(x_peers):
                     send(meta, metabuf.at[d], meta_send, meta_recv, device)
+                left(metabuf, meta_send)
                 half = pl.ds(0, SLOTS)
             for d, device in enumerate(x_peers):
                 send(prod.at[it, half], pbuf.at[it, d, half], px_send.at[it], px_recv.at[it, d], device)
+        left(pbuf.at[it], px_send.at[it])
         if it == 0:
-            for j, p in enumerate(PLANE_PEERS):
-                send(costrow, costbuf.at[j], cost_send, cost_recv, at_offset(p))
+            for j, device in enumerate(plane):
+                send(costrow, costbuf.at[j], cost_send, cost_recv, device)
+            left(costbuf, cost_send)
 
             def turn(i, _):
                 for u in range(UNROLL_T):
@@ -258,18 +270,25 @@
                 return 0
 
             lax.fori_loop(0, SLOTS // UNROLL_T, turn, 0)
-        total = scatter(hot3(col_ids, my_cols), prod[it])
         if it == 0:
+            hots[XN - 1] = hot3(col_ids, my_cols)
             wait_for(metabuf, meta_recv)
+            for d in range(XN - 1):
+                hots[d] = hot3(col_ids, metabuf[d, 0:1, :])
+            row_hot[...] = hot3(row_ids, my_rows)
+            new_hot[...] = hot3(row_ids, new_cols)
+        total = scatter(hots[XN - 1], prod[it])
         for d in (1, 2, 0):
             wait_for(pbuf.at[it, d], px_recv.at[it, d])
-            total = total + scatter(hot3(col_ids, metabuf[d, 0:1, :]), pbuf[it, d])
+            total = total + scatter(hots[d], pbuf[it, d])
         dense[it] = total
         send(dense.at[it], sib.at[it], sib_send.at[it], sib_recv.at[it], sibling)
+        left(sib.at[it], sib_send.at[it])
         if it == 0:
             dem4 = dem_sq + metabuf[0, 1:2, :] + metabuf[1, 1:2, :] + metabuf[2, 1:2, :]
             demrow[0] = dem4
             send(demrow.at[0], demrow.at[1], dem_send, dem_recv, sibling)
+            left(demrow.at[1], dem_send)
             wait_for(costbuf, cost_recv)
             cost_all = jnp.sum(costbuf[...], axis=0) + costrow[...]
             cost_total = jnp.sum(cost_all, axis=1, keepdims=True)
@@ -285,15 +304,13 @@
         xcur[...] = now
 
         products(0, SLOTS, UNROLL, block_tile(xtile, bcol_s), blk_t, prod8)
-        put_pairs(part.at[it], scatter(hot3(row_ids, my_rows), summed(prod8, 0, SLOTS)))
-        for j, p in enumerate(PLANE_PEERS):
-            target = at_offset(p)
-            ty, tz = target[1] // ZN, lax.rem(target[1], ZN)
-            at = pl.multiple_of((lax.rem(ty, 2) * 4 + lax.rem(tz, 4)) * CHUNK, CHUNK)
-            send(part.at[it, pl.ds(at, CHUNK)], rsbuf.at[it, j], rs_send.at[it], rs_recv.at[it], target)
+        put_pairs(part.at[it], scatter(row_hot[...], summed(prod8, 0, SLOTS)))
+        for j, device in enumerate(plane):
+            send(part.at[it, pl.ds(chunk_at[j], CHUNK)], rsbuf.at[it, j], rs_send.at[it], rs_recv.at[it], device)
+        left(rsbuf.at[it], rs_send.at[it])
         if it == ITERS - 1:
             put_pairs(primal_o, xcur[...])
-            put_primal = fetch(primal_o, primal_oh, out_sem.at[0])
+            pending.append(fetch(primal_o, primal_oh, out_sem.at[0]).wait)
         y_was = dual[pl.ds(my_at, CHUNK), :] if it == 0 else ybuf[it - 1, pl.ds(my_at, CHUNK), :]
         mine = part[it, pl.ds(my_at, CHUNK), :]
         wait_for(rsbuf.at[it], rs_recv.at[it])
@@ -302,19 +319,21 @@
         held = ybuf.at[it] if it < ITERS - 1 else yall.at[core, x]
         held[pl.ds(my_at, CHUNK), :] = y_now
         chunk = held.at[pl.ds(my_at, CHUNK)]
-        for p in NEAR_PEERS if it < ITERS - 1 else LAST_PEERS:
-            send(chunk, chunk, ag_send.at[it], ag_recv.at[it], at_offset(p))
+        peers = near if it < ITERS - 1 else last
+        for device in peers:
+            send(chunk, chunk, ag_send.at[it], ag_recv.at[it], device)
+        left(rsbuf.at[it, pl.ds(0, len(peers))], ag_send.at[it])
         if it < ITERS - 1:
             wait_for(held.at[pl.ds(0, len(NEAR_PEERS) * CHUNK)], ag_recv.at[it])
             put_tiles(ytile, pairs(held, ROWB))
 
-    new_hot = hot3(row_ids, new_cols)
     lane_row = lax.broadcasted_iota(jnp.int32, (8, EDGE), 0)
     fresh_copy.wait()
     wait_for(rsbuf.at[0], ag_recv.at[ITERS - 1])
     send(yall.at[core], yall.at[core], fs_send, fs_recv, sibling)
+    left(yall.at[core], fs_send)
     dual_o[...] = yall[core, x]
-    put_dual = fetch(dual_o, dual_oh, out_sem.at[1])
+    pending.append(fetch(dual_o, dual_oh, out_sem.at[1]).wait)
     wait_for(yall.at[core], fs_recv)
 
     yflat = yall.reshape(2 * XN * 2 * ROWB, LANES)
@@ -326,22 +345,12 @@
         return piece_tile(yflat, at, lane_row)
 
     products(0, NEW, UNROLL_NEW, new_tile, frs, prod8)
-    put_pairs(priced, scatter(new_hot, summed(prod8, 0, NEW)))
+    put_pairs(priced, scatter(new_hot[...], summed(prod8, 0, NEW)))
     reduced_o[...] = fcost[...] - priced[...]
-    put_reduced = fetch(reduced_o, reduced_oh, out_sem.at[2])
-
-    wait_for(yall.at[core], fs_send)
-    wait_for(metabuf, meta_send)
-    wait_for(costbuf, cost_send)
-    wait_for(demrow.at[1], dem_send)
-    for it in range(ITERS):
-        wait_for(pbuf.at[it], px_send.at[it])
-        wait_for(sib.at[it], sib_send.at[it])
-        wait_for(rsbuf.at[it], rs_send.at[it])
-        wait_for(rsbuf.at[it, pl.ds(0, len(NEAR_PEERS if it < ITERS - 1 else LAST_PEERS))], ag_send.at[it])
-    put_primal.wait()
-    put_dual.wait()
-    put_reduced.wait()
+    pending.append(fetch(reduced_o, reduced_oh, out_sem.at[2]).wait)
+
+    for done in pending:
+        done()
 
 
 def hand_over(*refs):
@@ -388,7 +397,8 @@
             f32(2, 8 * SLOTS, LANES),
             f32(ITERS, 2 * ROWB, LANES), f32(ITERS, PLANE - 1, CHUNK, LANES),
             f32(ITERS, 2 * ROWB, LANES), f32(2, XN, 2 * ROWB, LANES),
-            f32(2 * NEW, LANES),
+            f32(2 * NEW, LANES), pltpu.VMEM((XN, COLB, EDGE), BF),
+            pltpu.VMEM((ROWB, EDGE), BF), pltpu.VMEM((NEW, EDGE), BF),
             dma((13,)), dma((LOADS,)), dma,
             dma((ITERS,)), dma((ITERS, XN - 1)), dma, dma, dma, dma, dma, dma,
             dma((ITERS,)), dma((ITERS,)), dma((ITERS,)), dma((ITERS,)),

time: 56.2 us -> 56 us (level)
  no operation moved by 1% of the time
where the time goes in v4:
time: 56 us; the launch traced here: 55.8 us
  Pallas kernels  53.9 us (96%)
  between operations  1.93 us (3%)
    pallas_call x1, Pallas kernels, local(): pl.pallas_call(kernel, out_shape=tuple((jax.ShapeDtypeStruct((n, LANES),...  52.2 us
    pallas_call x1, Pallas kernels, local(): pl.pallas_call(hand_over, out_shape=tuple((jax.ShapeDtypeStruct(o.shape,...  1.63 us

profile of v4, /device:TPU:1, one launch (start us, length us, event | category | flops | bytes accessed | tf_op | source)
XLA Modules:
  0.0 55.8 jit_solution(1517381282052053339)
XLA Ops:
  1.9 52.2 %shard_map.148 = (f32[256,128]{1,0:T(8,128)}, f32[64,128]{1,0:T(8,128)}, f32[64,128]{1,0:T(8,128)}) custom-call(s32[48]{0:T(128)} %brow_h.1, s32[48]{0:T(128)} %bcol_h.1, s32[1]{0:T(128)S(6)} %copy.16.cnt_h, s32[32]{0:T(128)} %frow_h.1, f32[1]{0:T(128)S(6)} %copy.17.step_h, s32[1,48]{1,0:T(1,128)} %bitcast.17, s32[1,48]{1,0:T(1,128)} %bitcast.16, ...), custom_call_target="tpu_custom_call" | custom-call | tf_op jit(solution)/shard_map/pallas_call | solution.py:378
  54.2 1.6 %shard_map.149 = (f32[256,128]{1,0:T(8,128)}, f32[64,128]{1,0:T(8,128)}, f32[64,128]{1,0:T(8,128)}) custom-call(f32[256,128]{1,0:T(8,128)} %get-tuple-element.9.refs_0_, f32[64,128]{1,0:T(8,128)} %get-tuple-element.10.refs_1_, f32[64,128]{1,0:T(8,128)} %get-tuple-element.11.refs_2_), custom_call_target="tpu_custom_call" | custom-call | tf_op jit(solution)/shard_map/pallas_call | solution.py:416

commit v5 on v4

--- a/solution.py
+++ b/solution.py
@@ -10,7 +10,7 @@
 EDGE = 256
 LANES = 128
 SLOTS = 48
-HALF = SLOTS // 2
+THIRD = SLOTS // 3
 NEW = 32
 XN, YN, ZN = 4, 4, 8
 PLANE = YN * ZN
@@ -20,7 +20,7 @@
 PAD = 64
 BF = jnp.bfloat16
 F32 = jnp.float32
-LOADS = 4
+LOADS = 3
 UNROLL = 48
 UNROLL_NEW = 32
 UNROLL_T = 4
@@ -239,14 +239,14 @@
     tau = sigma = None
     fresh_copy = None
     for it in range(ITERS):
-        for h in range(2):
+        for h in range(LOADS):
             if it == 0:
-                for copy in loads[h * LOADS // 2:(h + 1) * LOADS // 2]:
+                for copy in loads[h:h + 1]:
                     copy.wait()
-            products(h * HALF, HALF, HALF, block_tile(ytile, brow_s), blk, prod8)
-            half = pl.ds(h * HALF, HALF)
-            prod[it, half, :] = summed(prod8, h * HALF, HALF)
-            if it == 0 and h == 0:
+            products(h * THIRD, THIRD, THIRD, block_tile(ytile, brow_s), blk, prod8)
+            half = pl.ds(h * THIRD, THIRD)
+            prod[it, half, :] = summed(prod8, h * THIRD, THIRD)
+            if it == 0 and h < LOADS - 1:
                 continue
             if it == 0:
                 fresh_copy = fetch(fresh, frs, fresh_sem)

time: 56 us -> 56.1 us (level)
  no operation moved by 1% of the time
where the time goes in v5:
time: 56.1 us; the launch traced here: 56 us
  Pallas kernels  54.1 us (96%)
  between operations  1.93 us (3%)
    pallas_call x1, Pallas kernels, local(): pl.pallas_call(kernel, out_shape=tuple((jax.ShapeDtypeStruct((n, LANES),...  52.4 us
    pallas_call x1, Pallas kernels, local(): pl.pallas_call(hand_over, out_shape=tuple((jax.ShapeDtypeStruct(o.shape,...  1.63 us

profile of v5, /device:TPU:1, one launch (start us, length us, event | category | flops | bytes accessed | tf_op | source)
XLA Modules:
  0.0 56.0 jit_solution(6075305212631896429)
XLA Ops:
  1.9 52.4 %shard_map.148 = (f32[256,128]{1,0:T(8,128)}, f32[64,128]{1,0:T(8,128)}, f32[64,128]{1,0:T(8,128)}) custom-call(s32[48]{0:T(128)} %brow_h.1, s32[48]{0:T(128)} %bcol_h.1, s32[1]{0:T(128)S(6)} %copy.16.cnt_h, s32[32]{0:T(128)} %frow_h.1, f32[1]{0:T(128)S(6)} %copy.17.step_h, s32[1,48]{1,0:T(1,128)} %bitcast.17, s32[1,48]{1,0:T(1,128)} %bitcast.16, ...), custom_call_target="tpu_custom_call" | custom-call | tf_op jit(solution)/shard_map/pallas_call | solution.py:378
  54.4 1.6 %shard_map.149 = (f32[256,128]{1,0:T(8,128)}, f32[64,128]{1,0:T(8,128)}, f32[64,128]{1,0:T(8,128)}) custom-call(f32[256,128]{1,0:T(8,128)} %get-tuple-element.9.refs_0_, f32[64,128]{1,0:T(8,128)} %get-tuple-element.10.refs_1_, f32[64,128]{1,0:T(8,128)} %get-tuple-element.11.refs_2_), custom_call_target="tpu_custom_call" | custom-call | tf_op jit(solution)/shard_map/pallas_call | solution.py:416
